TPU v7x, 256 devices: a whole 4x4x8 slice. The times are simulated.
256 devices in a mesh: dp: 16 (over y_lo, z), seq: 16 (over x, y_hi, core).
Axes of the slice: x: 4, y: 4 (y_hi: 2, y_lo: 2; y = y_hi * 2 + y_lo), z: 8, core: 2. Of those that a mesh axis runs over, the one named last changes fastest.
Arguments:
- tokens: bfloat16 [16, 4096, 1536], P('dp', 'seq'), may hold values from -64 to 64
- keep_index: int32 [16, 4096], P('dp', 'seq'), may hold values from 0 to 8191, as said below
- d_out: bfloat16 [16, 4096, 768], P('dp', 'seq'), may hold values from -6 to 6
- w_query: bfloat16 [1536, 768], replicated, may hold values from -0.15625 to 0.15625
- w_kv: bfloat16 [1536, 1536], replicated, may hold values from -0.15625 to 0.15625
- w_merge: float32 [4, 1536], replicated, may hold values from -2.5 to 2.5
Outputs:
- attended: bfloat16 [16, 4096, 768], P('dp', 'seq')
- grad_tokens: bfloat16 [16, 4096, 1536], P('dp', 'seq')
- grad_query_w: float32 [1536, 768], P('seq')
- grad_kv_w: float32 [1536, 1536], P('seq')
- grad_merge: float32 [4, 1536], P(None, 'seq')
Inputs may be any that keep to these rules, and one draw needn't show every extreme that they name: `keep_index`: for each image: ascending and distinct; made of whole aligned blocks of 128 positions, 32 of the 64 blocks, the first and the last block always among them.
All inputs are finite; a program needn't handle non-finite values.
Results may differ from a plain program's by a relative error of at most 0.034.
The roundings to bfloat16 on the way count: a program that leaves them out, or rounds other values in their place, can miss the bound.
Values may be sent and summed in bfloat16 or wider, within the bound.
No kernel may reach another device: no remote copies, remote signals or barrier semaphores. Data moves between devices by JAX's collectives and lax.ppermute only.
A program may use at most 128 MiB of HBM per device.

v0:
```python
import jax
import jax.numpy as jnp
from jax import lax
from jax.sharding import PartitionSpec as P

D = 1536
HEADS = 12
HEAD = 64
COARSE_W = 64


def rotate(values, rows, cols, sign):
    count = values.shape[0]
    quarter = HEAD // 4
    parts = values.reshape(count, HEADS, 4, quarter)
    freq = 100.0 ** (-jnp.arange(quarter, dtype=jnp.float32) / quarter)
    row_angle = (rows[:, None] * freq)[:, None, :]
    col_angle = (cols[:, None] * freq)[:, None, :]
    row_cos, row_sin = (jnp.cos(row_angle), sign * jnp.sin(row_angle))
    col_cos, col_sin = (jnp.cos(col_angle), sign * jnp.sin(col_angle))
    first, second, third, fourth = (parts[:, :, 0], parts[:, :, 1], parts[:, :, 2], parts[:, :, 3])
    turned = jnp.stack(
        [
            first * row_cos - second * row_sin,
            first * row_sin + second * row_cos,
            third * col_cos - fourth * col_sin,
            third * col_sin + fourth * col_cos,
        ],
        axis=2,
    )
    return turned.reshape(count, HEADS * HEAD)


def places(index):
    cell = index // 4
    inner = index % 4
    rows = (2 * (cell // COARSE_W) + inner // 2).astype(jnp.float32)
    cols = (2 * (cell % COARSE_W) + inner % 2).astype(jnp.float32)
    return (rows, cols)


def key_places(index):
    cell = index[::4] // 4
    rows = (2 * (cell // COARSE_W)).astype(jnp.float32) + 0.5
    cols = (2 * (cell % COARSE_W)).astype(jnp.float32) + 0.5
    return (rows, cols)


def on_device(tokens, keep_index, d_out, w_query, w_kv, w_merge):
    own = tokens[0]
    index = keep_index[0]
    grad = d_out[0]
    count = own.shape[0]
    cells = count // 4
    width = w_query.shape[1]
    scale = HEAD ** (-0.5)
    query_rows, query_cols = places(index)
    key_rows, key_cols = key_places(index)
    query = rotate(
        jnp.dot(own, w_query, preferred_element_type=jnp.float32), query_rows, query_cols, 1.0
    ).astype(jnp.bfloat16)
    quads = own.astype(jnp.float32).reshape(cells, 4, D)
    merged = jnp.sum(quads * w_merge[None], axis=1).astype(jnp.bfloat16)
    keyval = jnp.dot(merged, w_kv, preferred_element_type=jnp.float32)
    key = rotate(keyval[:, :width], key_rows, key_cols, 1.0).astype(jnp.bfloat16)
    value = keyval[:, width:].astype(jnp.bfloat16)
    query_h = query.reshape(count, HEADS, HEAD)
    grad_h = grad.reshape(count, HEADS, HEAD)
    top = jnp.full((HEADS, count), -1e30, jnp.float32)
    key_p = lax.all_gather(key, "seq", axis=0, tiled=True)
    value_p = lax.all_gather(value, "seq", axis=0, tiled=True)
    key_h = key_p.reshape(key_p.shape[0], HEADS, HEAD)
    value_h = value_p.reshape(value_p.shape[0], HEADS, HEAD)
    scores = jnp.einsum("qhd,khd->hqk", query_h, key_h, preferred_element_type=jnp.float32) * scale
    newtop = jnp.maximum(top, jnp.max(scores, axis=-1))
    expo = jnp.exp(scores - newtop[..., None])
    denom = jnp.sum(expo, axis=-1)
    total = jnp.einsum(
        "hqk,khd->hqd", expo.astype(jnp.bfloat16), value_h, preferred_element_type=jnp.float32
    )
    top, denom, total = (newtop, denom, total)
    mixed = total / denom[..., None]
    attended = jnp.transpose(mixed, (1, 0, 2)).reshape(count, width).astype(jnp.bfloat16)
    logsum = top + jnp.log(denom)
    delta = jnp.sum(
        attended.astype(jnp.float32).reshape(count, HEADS, HEAD) * grad_h.astype(jnp.float32),
        axis=-1,
    ).T
    key_p = lax.all_gather(key, "seq", axis=0, tiled=True)
    value_p = lax.all_gather(value, "seq", axis=0, tiled=True)
    rows = key_p.shape[0]
    key_h = key_p.reshape(rows, HEADS, HEAD)
    value_h = value_p.reshape(rows, HEADS, HEAD)
    scores = jnp.einsum("qhd,khd->hqk", query_h, key_h, preferred_element_type=jnp.float32) * scale
    prob = jnp.exp(scores - logsum[..., None])
    dprob = jnp.einsum("qhd,khd->hqk", grad_h, value_h, preferred_element_type=jnp.float32)
    dscore = (prob * (dprob - delta[..., None])).astype(jnp.bfloat16)
    dq_raw = jnp.einsum("hqk,khd->qhd", dscore, key_h, preferred_element_type=jnp.float32) * scale
    dkey = jnp.einsum("hqk,qhd->khd", dscore, query_h, preferred_element_type=jnp.float32) * scale
    dval = jnp.einsum(
        "hqk,qhd->khd", prob.astype(jnp.bfloat16), grad_h, preferred_element_type=jnp.float32
    )
    block = jnp.concatenate([dkey.reshape(rows, width), dval.reshape(rows, width)], axis=1)
    key_terms = block
    dq_raw, key_terms = (dq_raw, key_terms)
    dq = rotate(dq_raw.reshape(count, width), query_rows, query_cols, -1.0).astype(jnp.bfloat16)
    dkv_sum = lax.psum_scatter(
        key_terms.astype(jnp.bfloat16), "seq", scatter_dimension=0, tiled=True
    ).astype(jnp.float32)
    dkv = jnp.concatenate(
        [rotate(dkv_sum[:, :width], key_rows, key_cols, -1.0), dkv_sum[:, width:]], axis=1
    ).astype(jnp.bfloat16)
    dmerged = jnp.dot(dkv, w_kv.T, preferred_element_type=jnp.float32)
    back = jnp.dot(dq, w_query.T, preferred_element_type=jnp.float32)
    grad_tokens = (back + (w_merge[None] * dmerged[:, None, :]).reshape(count, D)).astype(
        jnp.bfloat16
    )
    term_q = jnp.dot(own.T, dq, preferred_element_type=jnp.float32)
    term_kv = jnp.dot(merged.T, dkv, preferred_element_type=jnp.float32)
    term_m = jnp.einsum("ctd,cd->dt", quads, dmerged)
    slice_q, slice_kv, slice_m = (
        lax.psum_scatter(
            term_q.astype(jnp.bfloat16), "seq", scatter_dimension=0, tiled=True
        ).astype(jnp.float32),
        lax.psum_scatter(
            term_kv.astype(jnp.bfloat16), "seq", scatter_dimension=0, tiled=True
        ).astype(jnp.float32),
        lax.psum_scatter(
            term_m.astype(jnp.bfloat16), "seq", scatter_dimension=0, tiled=True
        ).astype(jnp.float32),
    )
    total_q, total_kv, total_m = lax.psum((slice_q, slice_kv, slice_m), "dp")
    return (attended[None], grad_tokens[None], total_q, total_kv, total_m.T)


def solution(mesh):
    placed = (P("dp", "seq", None), P("dp", "seq"), P("dp", "seq", None), P(), P(), P())
    return jax.shard_map(
        on_device,
        mesh=mesh,
        in_specs=placed,
        out_specs=(
            P("dp", "seq", None),
            P("dp", "seq", None),
            P("seq", None),
            P("seq", None),
            P(None, "seq"),
        ),
        check_vma=False,
    )
```

profile of v0, /device:TPU:2, one launch (start us, length us, event | category | flops | bytes accessed | tf_op | source)
XLA Modules:
  0.0 575.1 jit_solution(4410430061931348485)
XLA Ops:
  7.2 0.8 slice.72
  8.1 1.7 squeeze.8
  9.8 2.0 multiply_reduce_fusion.2
  11.9 0.7 copy-done.12
  12.6 3.3 fusion.47
  15.9 0.7 copy-done.14
  16.6 0.7 slice.91
  17.3 1.1 copy.29
  18.4 0.7 broadcast_multiply_fusion.4
  19.1 0.1 subtract_convert_fusion.5
  19.2 0.1 pad_maximum_fusion.5
  19.3 0.5 copy-done.19
  19.7 0.8 copy.30
  20.6 1.6 slice.140
  22.2 0.2 reduce-scatter.13.cloned.1.call-start
  22.4 0.6 fusion.38
  23.0 0.6 fusion.37
  23.6 2.5 copy.28
  26.1 2.7 fusion.27
  28.9 0.8 broadcast_multiply_fusion.2
  29.7 0.2 copy.33
  29.9 0.1 subtract_convert_fusion.1
  30.1 0.2 copy-done.17
  30.3 44.8 %all-gather.3.cloned.1.call-done = bf16[1024,768]{1,0:T(8,128)(2,1)} async-done(((bf16[64,768]{1,0:T(8,128)(2,1)}), bf16[1024,768]{1,0:T(8,128)(2,1)}) %all-gather.3.cloned.1.call-update) | async-done | bytes 1572880 | tf_op jit(solution)/shard_map/all_gather | solution.py:70
  75.1 1.7 copy.31
  76.9 1.9 multiply_reduce_fusion
  78.8 2.7 fusion.1
  81.6 1.7 copy-done
  83.3 3.5 fusion.15
  86.8 42.3 %all-gather.5.cloned.1.call-done = bf16[1024,768]{1,0:T(8,128)(2,1)} async-done(((bf16[64,768]{1,0:T(8,128)(2,1)}), bf16[1024,768]{1,0:T(8,128)(2,1)}) %all-gather.5.cloned.1.call-update) | async-done | bytes 1572880 | tf_op jit(solution)/shard_map/all_gather | solution.py:71
  129.0 2.6 copy.32
  131.7 8.4 %multiply_reduce_fusion.3 = (f32[256,12]{0,1:T(8,128)S(1)}, bf16[256,12,64]{0,2,1:T(8,128)(2,1)}) fusion(bf16[256,12,64]{0,2,1:T(8,128)(2,1)} %bitcast.86, f32[256,12]{0,1:T(8,128)S(1)} %bitcast.96, bf16[1024,12,64]{0,2,1:T(8,128)(2,1)} %bitcast.77, f32[12,256,1024]{2,1,0:T(8,128)} %copy-done, f32[12,256]{1,0:T(8,128)S(1)} %broadcast_maximum_fusion), kind=kOutput, calls=%fused_computation.34 | convolution fusion | flops 413266944 | bytes 14979072 | tf_op jit(solution)/shard_map/hqk,khd->hqd/dot_general | solution.py:78
  140.0 0.5 copy-done.1
  140.5 5.5 fusion
  146.0 1.2 multiply_convert_fusion
  147.3 1.4 copy-done.2
  148.7 2.0 pad_maximum_fusion
  150.7 4.8 copy.45
  155.5 0.3 reduce-scatter.15.cloned.1.call-start
  155.8 4.8 convolution_multiply_fusion
  160.7 0.1 multiply_subtract_fusion.1
  160.9 0.8 fusion.12
  161.7 2.5 copy.47
  164.2 73.3 %reduce-scatter.13.cloned.1.call-done = bf16[64,1536]{1,0:T(8,128)(2,1)} async-done(((bf16[1024,1536]{1,0:T(8,128)(2,1)}), bf16[64,1536]{1,0:T(8,128)(2,1)}) %reduce-scatter.13.cloned.1.call-update) | async-done | bytes 196624
  237.5 1.0 fusion.46
  238.5 0.2 copy.51
  238.7 0.2 copy.52
  238.9 0.1 subtract_convert_fusion.3
  238.9 0.1 pad_maximum_fusion.6
  239.0 3.9 fusion.30
  242.9 0.4 multiply_reduce_fusion.1
  243.3 1.0 copy.49
  244.4 3.6 convolution_convert_fusion
  248.1 0.9 copy.35
  249.0 71.4 %reduce-scatter.15.cloned.1.call-done = bf16[96,768]{1,0:T(8,128)(2,1)} async-done(((bf16[1536,768]{1,0:T(8,128)(2,1)}), bf16[96,768]{1,0:T(8,128)(2,1)}) %reduce-scatter.15.cloned.1.call-update) | async-done | bytes 147472
  320.4 1.1 copy.48
  321.5 2.2 broadcast_multiply_fusion
  323.7 2.8 mul.550
  326.5 3.1 fusion.14
  329.6 66.7 %reduce-scatter.17.cloned.1.call-done = bf16[96,4]{1,0:T(8,128)(2,1)} async-done(((bf16[1536,4]{1,0:T(8,128)(2,1)}), bf16[96,4]{1,0:T(8,128)(2,1)}) %reduce-scatter.17.cloned.1.call-update) | async-done | bytes 784
  396.3 0.8 copy.54
  397.1 93.2 %reduce-scatter.11.cloned.1.call-done = bf16[96,1536]{1,0:T(8,128)(2,1)} async-done(((bf16[1536,1536]{1,0:T(8,128)(2,1)}), bf16[96,1536]{1,0:T(8,128)(2,1)}) %reduce-scatter.11.cloned.1.call-update) | async-done | bytes 294928 | tf_op jit(solution)/shard_map/reduce_scatter | solution.py:125
  490.3 77.2 %all-reduce.2 = (f32[96,768]{0,1:T(8,128)S(1)}, f32[96,1536]{1,0:T(8,128)}, f32[4,96]{1,0:T(4,128)}) all-reduce(bf16[96,768]{0,1:T(8,128)(2,1)S(1)} %copy.48, bf16[96,1536]{1,0:T(8,128)(2,1)} %reduce-scatter.11.cloned.1.call-done, f32[4,96]{1,0:T(4,128)S(1)} %bitcast.98), channel_id=1, replica_groups=mesh['dp'=16,'seq'=16] {'dp'}, use_global_device_ids=true, to_apply=%region_6.7 | all-reduce | flops 221568 | bytes 1330176 | tf_op jit(solution)/shard_map/psum | solution.py:132
  567.4 0.9 copy.36
  (75 shorter events, 0.6 us)
Async XLA Ops:
  7.2 68.0 %all-gather.3.cloned.1.call-start = ((), (), s32[]{:S(2)}) async-start(), calls=%async_computation.4 | async-start | bytes 1671168 | tf_op jit(solution)/shard_map/all_gather | solution.py:70
  7.2 12.0 %copy-start.30 = (f32[16]{0:T(128)}, f32[16]{0:T(128)S(1)}, u32[]{:S(2)}) copy-start(f32[16]{0:T(128)S(1)} %multiply_power_fusion) | copy-start | bytes 196
  9.8 16.3 %copy-start.7 = (bf16[64,4,1536]{2,1,0:T(4,128)(2,1)}, bf16[64,4,1536]{2,1,0:T(4,128)(2,1)S(1)}, u32[]{:S(2)}) copy-start(bf16[64,4,1536]{2,1,0:T(4,128)(2,1)S(1)} %squeeze.8) | copy-start | bytes 2359300
  9.8 12.6 %copy-start.29 = (s32[1,256]{1,0:T(1,128)S(1)}, s32[1,256]{1,0:T(1,128)}, u32[]{:S(2)}) copy-start(s32[1,256]{1,0:T(1,128)} %param.7) | copy-start | bytes 3076
  9.8 13.7 %copy-start.5 = (bf16[1536,768]{1,0:T(8,128)(2,1)S(1)}, bf16[1536,768]{1,0:T(8,128)(2,1)}, u32[]{:S(2)}) copy-start(bf16[1536,768]{1,0:T(8,128)(2,1)} %param.9) | copy-start | bytes 7077892
  11.9 0.7 copy-start.12
  15.8 0.7 copy-start.14
  19.1 0.6 copy-start.19
  19.1 0.6 copy-start.21
  20.5 108.5 %all-gather.5.cloned.1.call-start = ((), (), s32[]{:S(2)}) async-start(), calls=%async_computation.5 | async-start | bytes 1671168 | tf_op jit(solution)/shard_map/all_gather | solution.py:71
  22.2 215.3 %reduce-scatter.13.cloned.1.call-start = ((), (), s32[]{:S(2)}) async-start(), calls=%async_computation.7 | async-start | bytes 3342336
  23.6 6.1 %copy-start.15 = (bf16[1,256,768]{2,1,0:T(8,128)(2,1)S(1)}, bf16[1,256,768]{2,1,0:T(8,128)(2,1)}, u32[]{:S(2)}) copy-start(bf16[1,256,768]{2,1,0:T(8,128)(2,1)} %param.8) | copy-start | bytes 1179652
  26.1 2.8 copy-start.27
  26.1 2.8 copy-start.28
  26.1 2.8 copy-start.31
  29.7 0.6 copy-start.17
  29.9 51.7 %copy-start.10 = (bf16[1,256,768]{1,2,0:T(8,128)(2,1)}, bf16[1,256,768]{1,2,0:T(8,128)(2,1)S(1)}, u32[]{:S(2)}) copy-start(bf16[1,256,768]{1,2,0:T(8,128)(2,1)S(1)} %copy.33) | copy-start | bytes 1179652
  76.8 1.9 copy-start.3
  78.8 4.5 copy-start
  131.6 8.9 %copy-start.1 = (f32[12,256,1024]{2,1,0:T(8,128)S(1)}, f32[12,256,1024]{2,1,0:T(8,128)}, u32[]{:S(2)}) copy-start(f32[12,256,1024]{2,1,0:T(8,128)} %copy-done) | copy-start | bytes 37748740
  146.0 2.7 copy-start.2
  146.0 2.7 copy-start.9
  150.7 5.1 copy-start.4
  155.5 5.1 copy-start.18
  155.5 5.1 copy-start.23
  155.5 5.1 copy-start.24
  155.5 5.3 copy-start.11
  155.5 164.9 %reduce-scatter.15.cloned.1.call-start = ((), (), s32[]{:S(2)}) async-start(), calls=%async_computation.8 | async-start | bytes 2506752
  161.6 77.2 %copy-start.20 = (f32[64,16]{0,1:T(8,128)S(1)}, f32[64,16]{0,1:T(8,128)}, u32[]{:S(2)}) copy-start(f32[64,16]{0,1:T(8,128)} %copy-done.19) | copy-start | bytes 12292
  161.6 77.2 %copy-start.22 = (f32[64,16]{0,1:T(8,128)S(1)}, f32[64,16]{0,1:T(8,128)}, u32[]{:S(2)}) copy-start(f32[64,16]{0,1:T(8,128)} %copy-done.21) | copy-start | bytes 12292
  161.7 77.2 %copy-start.25 = (f32[64,16]{0,1:T(8,128)S(1)}, f32[64,16]{0,1:T(8,128)}, u32[]{:S(2)}) copy-start(f32[64,16]{0,1:T(8,128)} %get-tuple-element.59) | copy-start | bytes 12292
  161.7 77.2 %copy-start.26 = (f32[64,16]{0,1:T(8,128)S(1)}, f32[64,16]{0,1:T(8,128)}, u32[]{:S(2)}) copy-start(f32[64,16]{0,1:T(8,128)} %get-tuple-element.70) | copy-start | bytes 12292
  164.1 78.7 %copy-start.8 = (bf16[64,4,1536]{2,1,0:T(4,128)(2,1)S(1)}, bf16[64,4,1536]{2,1,0:T(4,128)(2,1)}, u32[]{:S(2)}) copy-start(bf16[64,4,1536]{2,1,0:T(4,128)(2,1)} %copy-done.7) | copy-start | bytes 2359300
  164.2 232.1 %reduce-scatter.17.cloned.1.call-start = ((), (), s32[]{:S(2)}) async-start(), calls=%async_computation.9 | async-start | bytes 417792
  238.6 5.8 %copy-start.13 = (bf16[64,1536]{1,0:T(8,128)(2,1)S(1)}, bf16[64,1536]{1,0:T(8,128)(2,1)}, u32[]{:S(2)}) copy-start(bf16[64,1536]{1,0:T(8,128)(2,1)} %copy-done.12) | copy-start | bytes 589828
  244.4 3.7 copy-start.16
  244.4 245.9 %reduce-scatter.11.cloned.1.call-start = ((), (), s32[]{:S(2)}) async-start(), calls=%async_computation.6 | async-start | bytes 5013504 | tf_op jit(solution)/shard_map/reduce_scatter | solution.py:125
  248.0 78.5 %copy-start.6 = (bf16[1536,768]{1,0:T(8,128)(2,1)S(1)}, bf16[1536,768]{1,0:T(8,128)(2,1)}, u32[]{:S(2)}) copy-start(bf16[1536,768]{1,0:T(8,128)(2,1)} %param.9) | copy-start | bytes 7077892
Sparse Core Ops, SparseCore 0:
  20.6 54.4 all-gather.2
  78.4 50.6 all-gather.4
  155.6 81.8 reduce-scatter.12
  241.6 78.7 reduce-scatter.14
  324.3 71.9 reduce-scatter.16
  400.5 89.7 reduce-scatter.10
where the time goes:
time: 576 us; the launch traced here: 575 us
  waiting for transfers between devices  392 us (68%)
  blocking collectives  77.2 us (13%)
  matrix products  42.6 us (7%)
  local copies, waits for them, and re-layouts  35.5 us (6%)
  between operations  14.6 us (3%)
  other arithmetic  12.8 us (2%)
    unnamed x9, waiting for transfers between devices  211 us
    reduce_scatter x1, waiting for transfers between devices, on_device(): lax.psum_scatter(term_kv.astype(jnp.bfloat16), 'seq', scatter_dimension=0...  93.2 us
    psum x1, blocking collectives, on_device(): total_q, total_kv, total_m = lax.psum((slice_q, slice_kv, slice_m), 'dp')  77.2 us
    all_gather x1, waiting for transfers between devices, on_device(): key_p = lax.all_gather(key, 'seq', axis=0, tiled=True)  44.8 us
    all_gather x1, waiting for transfers between devices, on_device(): value_p = lax.all_gather(value, 'seq', axis=0, tiled=True)  42.3 us
    unnamed x75, local copies, waits for them, and re-layouts  20.8 us
  transfers between devices with their start and end apart: 6, of which 6 were waited for; matrix products, arithmetic and copies ran while one was open for 8% of the time, Pallas kernels for 0%

commit v1 on v0

v1 whole, which is shorter than its diff:
```python
import jax
import jax.numpy as jnp
import numpy as np
from jax import lax
from jax.experimental import pallas as pl
from jax.experimental.pallas import tpu as pltpu
from jax.sharding import PartitionSpec as P

D = 1536
HD = 768
HEADS = 12
HEAD = 64
GROUP = 192
ROWS = 384
TOK = 256
CELLS = 64
MSG = 400
FREQ = (100.0 ** (-np.arange(16, dtype=np.float64) / 16)).astype(np.float32)
F32 = jnp.float32
BF16 = jnp.bfloat16
VMEM_LIMIT = 56 * 1024 * 1024

X_SHIFT = [[(i, (((i >> 2) + k) % 4) * 4 + (i & 3)) for i in range(16)] for k in range(4)]
Y_SWAP = [(i, i ^ 2) for i in range(16)]
CORE_SWAP = [(i, i ^ 1) for i in range(16)]
YLO_SWAP = [(i, i ^ 8) for i in range(16)]
Z_GROUPS = [list(range(8)), list(range(8, 16))]


def params():
    return pltpu.CompilerParams(vmem_limit_bytes=VMEM_LIMIT)


def vmem():
    return pl.BlockSpec(memory_space=pltpu.VMEM)


def smem():
    return pl.BlockSpec(memory_space=pltpu.SMEM)


def mm(a, b, dims=((1,), (0,))):
    return lax.dot_general(a, b, (dims, ((), ())), preferred_element_type=F32)


def lane_tables(row, col, sign):
    lane = lax.broadcasted_iota(jnp.int32, row.shape, 1)
    angle = jnp.where((lane & 63) < 32, row, col)
    even = (lane & 31) < 16
    return jnp.cos(angle), jnp.sin(angle) * jnp.where(even, -sign, sign), even


def turn(u, cos, sin, even):
    swapped = jnp.where(even, pltpu.roll(u, 112, 1), pltpu.roll(u, 16, 1))
    return u * cos + swapped * sin


def merge(tokf, wm_ref, k, cells):
    total = None
    for t in range(4):
        one = tokf[k, pl.ds(t, cells, stride=4), :] * wm_ref[t : t + 1, pl.ds(128 * k, 128)]
        total = one if total is None else total + one
    return total


def keyval_kernel(x_ref, idx_ref, freq_ref, tok_ref, wm_ref, wkv_ref, o0, o1, o2, o3, tokf, merged, part, piece):
    j = pl.program_id(0)

    @pl.when(j == 0)
    def _():
        for k in range(12):
            tokf[k] = tok_ref[:, pl.ds(128 * k, 128)].astype(F32)
            merged[:, pl.ds(128 * k, 128)] = merge(tokf, wm_ref, k, CELLS).astype(BF16)

    part[j] = mm(merged[...], wkv_ref[...])

    @pl.when(j == 5)
    def _():
        i = lax.broadcasted_iota(jnp.int32, (CELLS, 128), 0)
        first = idx_ref[0] // 4
        second = idx_ref[128] // 4
        cell = jnp.where(i < 32, first + i, second + i - 32)
        row = (2 * (cell >> 6)).astype(F32) + 0.5
        col = (2 * (cell & 63)).astype(F32) + 0.5
        cos, sin, even = lane_tables(row * freq_ref[...], col * freq_ref[...], 1.0)
        left = lax.broadcasted_iota(jnp.int32, (CELLS, 128), 1) < 64
        for k in range(6):
            lanes = pl.ds(128 * (k % 2), 128)
            key = turn(part[k // 2, :, lanes], cos, sin, even)
            val = part[3 + k // 2, :, lanes]
            a = jnp.where(left, key, pltpu.roll(val, 64, 1)).astype(BF16)
            b = jnp.where(left, pltpu.roll(key, 64, 1), val).astype(BF16)
            piece[(2 * k) // 3, (2 * k) % 3] = a
            piece[(2 * k + 1) // 3, (2 * k + 1) % 3] = b
        x = x_ref[0]
        for d, out in enumerate((o0, o1, o2, o3)):
            out[...] = piece[(x + d) % 4]


def keyval(xs, index, freq, tokens, w_merge, w_kv):
    out = jax.ShapeDtypeStruct((3, CELLS, 128), BF16)
    whole = lambda shape: pl.BlockSpec(shape, lambda j: (0,) * len(shape))
    return pl.pallas_call(
        keyval_kernel,
        grid=(6,),
        in_specs=[
            smem(),
            smem(),
            whole((1, 128)),
            whole((TOK, D)),
            whole((4, D)),
            pl.BlockSpec((D, 256), lambda j: (0, j)),
        ],
        out_specs=[whole((3, CELLS, 128))] * 4,
        out_shape=[out] * 4,
        scratch_shapes=[
            pltpu.VMEM((12, TOK, 128), F32),
            pltpu.VMEM((CELLS, D), BF16),
            pltpu.VMEM((6, CELLS, 256), F32),
            pltpu.VMEM((4, 3, CELLS, 128), BF16),
        ],
        compiler_params=params(),
        name="keyval",
    )(xs, index, freq, tokens, w_merge, w_kv)


def sub_tables(row, col, freq):
    return (
        jnp.cos(row * freq),
        jnp.sin(row * freq),
        jnp.cos(col * freq),
        jnp.sin(col * freq),
    )


def sub_turn(u, tables, sign):
    rc, rs, cc, cs = tables
    a, b, c, d = u[0:16], u[16:32], u[32:48], u[48:64]
    return jnp.concatenate(
        [
            a * rc - sign * (b * rs),
            sign * (a * rs) + b * rc,
            c * cc - sign * (d * cs),
            sign * (c * cs) + d * cc,
        ],
        axis=0,
    )


def query_kernel(x_ref, idx_ref, freq_ref, tok_ref, wq_ref, do_ref, o0, o1, o2, o3, scr):
    index = idx_ref[...]
    cell = index >> 2
    row = 2 * (cell >> 6) + ((index >> 1) & 1)
    col = 2 * (cell & 63) + (index & 1)
    row = row.astype(F32)
    col = col.astype(F32)
    tables = sub_tables(row, col, freq_ref[...])
    query = mm(tok_ref[...], wq_ref[...]).T
    grad = do_ref[...].astype(F32).T
    line = lax.broadcasted_iota(jnp.int32, (16, TOK), 0)
    place = jnp.where(line == 0, row, jnp.where(line == 1, col, 0.0)).astype(BF16)
    for h in range(HEADS):
        g, k = h // 3, h % 3
        scr[g, pl.ds(64 * k, 64), :] = (sub_turn(query[64 * h : 64 * h + 64], tables, 1.0) * 0.125).astype(BF16)
    for g in range(4):
        scr[g, pl.ds(GROUP, GROUP), :] = grad[GROUP * g : GROUP * g + GROUP].astype(BF16)
        scr[g, pl.ds(2 * GROUP, 16), :] = place
    x = x_ref[0]
    for d, out in enumerate((o0, o1, o2, o3)):
        out[...] = scr[(x + d) % 4]


def queries(xs, index, freq, tokens, w_query, grad):
    out = jax.ShapeDtypeStruct((MSG, TOK), BF16)
    return pl.pallas_call(
        query_kernel,
        in_specs=[smem()] + [vmem()] * 5,
        out_specs=[vmem()] * 4,
        out_shape=[out] * 4,
        scratch_shapes=[pltpu.VMEM((4, MSG, TOK), BF16)],
        compiler_params=params(),
        name="queries",
    )(xs, index, freq, tokens, w_query, grad)


def attention_kernel(
    x_ref, freq_ref, q0, q1, q2, q3, u0, u1, u2, u3, a0, a1, a2, a3, dq_ref, keep_ref, send_ref, kvn, kvt, qd, att, acc
):
    x = x_ref[0]
    for k, u in enumerate((u0, u1, u2, u3)):
        for d in range(4):
            for h in range(3):
                kvn[h, pl.ds(256 * k + 64 * d, 64), :] = u[d, h]
    for h in range(3):
        kvt[h] = kvn[h].astype(F32).T.astype(BF16)
    for d, q in enumerate((q0, q1, q2, q3)):
        qd[d] = q[...]

    def step(i, carry):
        h = i // 4
        p = i % 4
        kv = kvn[h]
        kv_t = kvt[h]
        at = pl.ds(pl.multiple_of(64 * h, 64), 64)
        q = qd[p, at, :]
        do = qd[p, pl.ds(pl.multiple_of(GROUP + 64 * h, 64), 64), :]
        zero = jnp.zeros_like(q)
        q_pad = jnp.concatenate([q, zero], axis=0)
        do_pad = jnp.concatenate([zero, do], axis=0)
        scores = mm(kv, q_pad)
        top = jnp.max(scores, axis=0, keepdims=True)
        expo = jnp.exp(scores - top)
        denom = jnp.sum(expo, axis=0, keepdims=True)
        inv = 1.0 / denom
        mixed = mm(kv_t[64:128], expo.astype(BF16)) * inv
        mixed = mixed.astype(BF16)
        att[p, at, :] = mixed
        delta = jnp.sum(mixed.astype(F32) * do.astype(F32), axis=0, keepdims=True)
        prob = expo * inv
        dprob = mm(kv, do_pad)
        dscore = (prob * (dprob - delta)).astype(BF16)
        dq = mm(kv_t[0:64], dscore) * 0.125
        place = qd[p, pl.ds(2 * GROUP, 16), :].astype(F32)
        tables = sub_tables(place[0:1], place[1:2], freq_ref[...])
        dq_ref[(x + 4 - p) % 4, at, :] = sub_turn(dq, tables, -1.0).astype(BF16)
        part = mm(dscore, q_pad, ((1,), (1,))) + mm(prob.astype(BF16), do_pad, ((1,), (1,)))

        @pl.when(p == 0)
        def _():
            acc[...] = part

        @pl.when(p > 0)
        def _():
            acc[...] += part

        @pl.when(p == 3)
        def _():
            keep_ref[h] = acc[0:512]
            send_ref[h] = acc[512:1024].astype(BF16)

        return carry

    lax.fori_loop(0, 12, step, 0)
    for d, a in enumerate((a0, a1, a2, a3)):
        a[...] = att[d]


def attention(xs, freq, qs, us):
    out = jax.ShapeDtypeStruct((GROUP, TOK), BF16)
    return pl.pallas_call(
        attention_kernel,
        in_specs=[smem()] + [vmem()] * 9,
        out_specs=[vmem()] * 7,
        out_shape=[out] * 4
        + [
            jax.ShapeDtypeStruct((4, GROUP, TOK), BF16),
            jax.ShapeDtypeStruct((3, 512, 128), F32),
            jax.ShapeDtypeStruct((3, 512, 128), BF16),
        ],
        scratch_shapes=[
            pltpu.VMEM((3, 1024, 128), BF16),
            pltpu.VMEM((3, 128, 1024), BF16),
            pltpu.VMEM((4, MSG, TOK), BF16),
            pltpu.VMEM((4, GROUP, TOK), BF16),
            pltpu.VMEM((1024, 128), F32),
        ],
        compiler_params=params(),
        name="attention",
    )(xs, freq, *qs, *us)


def dkv_kernel(x_ref, freq_ref, q0, q1, q2, q3, keep_ref, core_ref, y_ref, out_ref):
    x = x_ref[0]
    i = lax.broadcasted_iota(jnp.int32, (32, 128), 0).astype(F32)
    left = lax.broadcasted_iota(jnp.int32, (32, 128), 1) < 64
    for d, q in enumerate((q0, q1, q2, q3)):
        place = q[pl.ds(2 * GROUP, 16), :].astype(F32)
        for b in range(2):
            row = jnp.broadcast_to(place[0:1, 128 * b : 128 * b + 1], (32, 128)) + 0.5
            col = jnp.broadcast_to(place[1:2, 128 * b : 128 * b + 1], (32, 128)) + 0.5 + 2.0 * i
            cos, sin, even = lane_tables(row * freq_ref[...], col * freq_ref[...], -1.0)
            at = pl.ds(64 * d + 32 * b, 32)
            for h in range(3):
                total = keep_ref[h, at, :] + core_ref[h, at, :].astype(F32) + y_ref[h, at, :].astype(F32)
                total = jnp.where(left, turn(total, cos, sin, even), total)
                out_ref[(x + 4 - d) % 4, h, pl.ds(32 * b, 32), :] = total.astype(BF16)


def finish_dkv(xs, freq, qs, keep, core, y):
    return pl.pallas_call(
        dkv_kernel,
        in_specs=[smem()] + [vmem()] * 8,
        out_specs=vmem(),
        out_shape=jax.ShapeDtypeStruct((4, 3, CELLS, 128), BF16),
        compiler_params=params(),
        name="finish_dkv",
    )(xs, freq, *qs, keep, core, y)


def term_q_kernel(x_ref, t0, t1, t2, t3, d0, d1, d2, d3, out_ref, scr):
    x = x_ref[0]
    toks = (t0, t1, t2, t3)
    for e, dq in enumerate((d0, d1, d2, d3)):
        total = None
        for d in range(4):
            one = mm(dq[(x + 4 - d) % 4], toks[d][...])
            total = one if total is None else total + one
        scr[(x + 4 - e) % 4] = total
    full = jnp.concatenate([scr[0], scr[1], scr[2], scr[3]], axis=0).T
    for r in range(4):
        out_ref[r] = full[96 * r : 96 * r + 96]


def term_q(xs, toks, dqs):
    return pl.pallas_call(
        term_q_kernel,
        in_specs=[smem()] + [vmem()] * 8,
        out_specs=vmem(),
        out_shape=jax.ShapeDtypeStruct((4, 96, HD), F32),
        scratch_shapes=[pltpu.VMEM((4, GROUP, ROWS), F32)],
        compiler_params=params(),
        name="term_q",
    )(xs, *toks, *dqs)


def natural(tiles, rows, put):
    left = lax.broadcasted_iota(jnp.int32, (rows, 128), 1) < 64
    for k in range(6):
        a = tiles(2 * k).astype(F32)
        b = tiles(2 * k + 1).astype(F32)
        put(128 * k, jnp.where(left, a, pltpu.roll(b, 64, 1)).astype(BF16))
        put(HD + 128 * k, jnp.where(left, pltpu.roll(a, 64, 1), b).astype(BF16))


def term_kv_kernel(x_ref, c_ref, t0, t1, t2, t3, k0, k1, k2, k3, tq_ref, wm_ref, wkv_ref, keep_ref, send_ref, m_ref, tokf, tiles, dkv, full):
    x = x_ref[0]
    c = c_ref[0]
    for d, t in enumerate((t0, t1, t2, t3)):
        for k in range(3):
            tokf[k, pl.ds(256 * d, 256), :] = t[:, pl.ds(128 * k, 128)].astype(F32)
    merged = jnp.concatenate([merge(tokf, wm_ref, k, 256) for k in range(3)], axis=1).astype(BF16)
    for e, k in enumerate((k0, k1, k2, k3)):
        group = (x + 4 - e) % 4
        for d in range(4):
            for h in range(3):
                tiles[group * 3 + h, pl.ds(64 * d, 64), :] = k[(x + 4 - d) % 4, h]

    def put(at, value):
        dkv[:, pl.ds(at, 128)] = value

    natural(lambda h: tiles[h], 256, put)
    grad = dkv[...]
    term = mm(merged, grad, ((0,), (0,)))
    for r in range(4):
        full[r, :, pl.ds(0, HD)] = tq_ref[r]
        full[r, :, pl.ds(HD, D)] = term[96 * r : 96 * r + 96]
    for h in range(2):
        keep_ref[h] = full[2 * h + c]
        send_ref[h] = full[2 * h + 1 - c].astype(BF16)
    dmerged = mm(grad, wkv_ref[...], ((1,), (1,)))
    for t in range(4):
        for k in range(3):
            one = dmerged[:, 128 * k : 128 * k + 128] * tokf[k, pl.ds(t, 256, stride=4), :]
            m_ref[t : t + 1, pl.ds(128 * k, 128)] = jnp.sum(one, axis=0, keepdims=True)
    m_ref[4:8, :] = jnp.zeros((4, ROWS), F32)


def term_kv(xs, cs, toks, dkvs, tq, w_merge, w_kv):
    spec = lambda shape: pl.BlockSpec(shape, lambda i, x, c: (0,) * len(shape))
    grid_spec = pltpu.PrefetchScalarGridSpec(
        num_scalar_prefetch=2,
        grid=(1,),
        in_specs=[spec((TOK, ROWS))] * 4
        + [spec((4, 3, CELLS, 128))] * 4
        + [
            spec((4, 96, HD)),
            pl.BlockSpec((4, ROWS), lambda i, x, c: (0, x[0])),
            pl.BlockSpec((ROWS, D), lambda i, x, c: (x[0], 0)),
        ],
        out_specs=[spec((2, 96, HD + D)), spec((2, 96, HD + D)), spec((8, ROWS))],
        scratch_shapes=[
            pltpu.VMEM((3, 1024, 128), F32),
            pltpu.VMEM((12, 256, 128), BF16),
            pltpu.VMEM((256, D), BF16),
            pltpu.VMEM((4, 96, HD + D), F32),
        ],
    )
    return pl.pallas_call(
        term_kv_kernel,
        grid_spec=grid_spec,
        out_shape=[
            jax.ShapeDtypeStruct((2, 96, HD + D), F32),
            jax.ShapeDtypeStruct((2, 96, HD + D), BF16),
            jax.ShapeDtypeStruct((8, ROWS), F32),
        ],
        compiler_params=params(),
        name="term_kv",
    )(xs, cs, *toks, *dkvs, tq, w_merge, w_kv)


def grad_tokens_kernel(x_ref, d0, d1, d2, d3, k0, k1, k2, k3, wq_ref, wkv_ref, wm_ref, out_ref, tiles, dkv, dqs, back):
    x = x_ref[0]
    for e, (q, k) in enumerate(((d0, k0), (d1, k1), (d2, k2), (d3, k3))):
        group = (x + 4 - e) % 4
        dqs[group] = q[0]
        for h in range(3):
            tiles[group * 3 + h] = k[0, h]

    def put(at, value):
        dkv[:, pl.ds(at, 128)] = value

    natural(lambda h: tiles[h], CELLS, put)
    dq = jnp.concatenate([dqs[g].astype(F32).T.astype(BF16) for g in range(4)], axis=1)
    full = mm(dq, wq_ref[...], ((1,), (1,)))
    dmerged = mm(dkv[...], wkv_ref[...], ((1,), (1,)))
    for k in range(12):
        lanes = pl.ds(128 * k, 128)
        back[k] = full[:, 128 * k : 128 * k + 128]
        for t in range(4):
            at = pl.ds(t, CELLS, stride=4)
            back[k, at, :] = back[k, at, :] + wm_ref[t : t + 1, lanes] * dmerged[:, 128 * k : 128 * k + 128]
        out_ref[0, :, lanes] = back[k].astype(BF16)


def grad_of_tokens(xs, dqs, dkvs, w_query, w_kv, w_merge):
    spec = lambda shape: pl.BlockSpec(shape, lambda i, x: (0,) * len(shape))
    grid_spec = pltpu.PrefetchScalarGridSpec(
        num_scalar_prefetch=1,
        grid=(1,),
        in_specs=[pl.BlockSpec((1, GROUP, TOK), lambda i, x: (x[0], 0, 0))] * 4
        + [pl.BlockSpec((1, 3, CELLS, 128), lambda i, x: (x[0], 0, 0, 0))] * 4
        + [spec((D, HD)), spec((D, D)), spec((4, D))],
        out_specs=spec((1, TOK, D)),
        scratch_shapes=[
            pltpu.VMEM((12, CELLS, 128), BF16),
            pltpu.VMEM((CELLS, D), BF16),
            pltpu.VMEM((4, GROUP, TOK), BF16),
            pltpu.VMEM((12, TOK, 128), F32),
        ],
    )
    return pl.pallas_call(
        grad_tokens_kernel,
        grid_spec=grid_spec,
        out_shape=jax.ShapeDtypeStruct((1, TOK, D), BF16),
        compiler_params=params(),
        name="grad_tokens",
    )(xs, *dqs, *dkvs, w_query, w_kv, w_merge)


def spread_x(parts):
    return [parts[0]] + [lax.ppermute(parts[k], "seq", X_SHIFT[k]) for k in range(1, 4)]


def on_device(tokens, keep_index, d_out, w_query, w_kv, w_merge):
    own = tokens[0]
    place = lax.axis_index("seq")
    x = place // 4
    y = (place // 2) % 2
    c = place % 2
    xs = x.reshape(1)
    cs = c.reshape(1)
    lane_freq = jnp.asarray(np.tile(FREQ, 8)[None, :])
    sub_freq = jnp.asarray(np.broadcast_to(FREQ[:, None], (16, TOK)).copy())

    parts = keyval(xs, keep_index[0], lane_freq, own, w_merge, w_kv)
    unit = jnp.stack(spread_x(parts))
    unit_c = lax.ppermute(unit, "seq", CORE_SWAP)
    unit_y = lax.ppermute(unit, "seq", Y_SWAP)
    unit_cy = lax.ppermute(unit_y, "seq", CORE_SWAP)
    qs = spread_x(queries(xs, keep_index, sub_freq, own, w_query, d_out[0]))

    held = lax.optimization_barrier((own, unit_y))[0]
    slices = [lax.dynamic_slice(held, (0, ROWS * ((x + k) % 4)), (TOK, ROWS)) for k in range(4)]
    toks = spread_x(slices)

    a0, a1, a2, a3, dq, keep, send = attention(xs, sub_freq, qs, [unit, unit_y, unit_c, unit_cy])
    core = lax.ppermute(send, "seq", CORE_SWAP)
    other = (keep[:, 256:] + core[:, 256:].astype(F32)).astype(BF16)
    from_y = lax.ppermute(other, "seq", Y_SWAP)
    dqs = [dq] + [lax.ppermute(dq, "seq", X_SHIFT[k]) for k in range(1, 4)]
    dkv = finish_dkv(xs, lane_freq, qs, keep, core, from_y)
    dkvs = [dkv] + [lax.ppermute(dkv, "seq", X_SHIFT[k]) for k in range(1, 4)]

    back = [a0] + [lax.ppermute(a, "seq", X_SHIFT[4 - k]) for k, a in ((1, a1), (2, a2), (3, a3))]
    order = jnp.stack(back)
    att = jnp.concatenate([lax.dynamic_index_in_dim(order, (g + 4 - x) % 4, 0, False) for g in range(4)], axis=0)
    attended = att.T

    tq = term_q(xs, toks, dqs)
    keep, send, m = term_kv(xs, cs, toks, dkvs, tq, w_merge, w_kv)
    got = lax.ppermute(send, "seq", CORE_SWAP)
    m = m + lax.ppermute(m, "seq", CORE_SWAP)
    summed = keep + got.astype(F32)
    mine = lax.dynamic_index_in_dim(summed, y, 0, False)
    theirs = lax.dynamic_index_in_dim(summed, 1 - y, 0, False).astype(BF16)
    got = lax.ppermute(theirs, "seq", Y_SWAP)
    m = m + lax.ppermute(m, "seq", Y_SWAP)
    mine = (mine + got.astype(F32)).astype(BF16)
    chunks = mine.reshape(4, 24, 2, 1152).transpose(0, 2, 1, 3).reshape(8, 24, 1152)
    m = lax.dynamic_slice(m, (0, 96 * (2 * y + c)), (8, 96)).astype(BF16)
    m = jnp.pad(m, ((0, 0), (0, 1152 - 96)))
    chunks = jnp.concatenate([chunks, jnp.broadcast_to(m[None], (8, 8, 1152))], axis=1)
    got = lax.all_to_all(chunks, "dp", 0, 0, axis_index_groups=Z_GROUPS)
    shard = jnp.sum(got.astype(F32), axis=0).astype(BF16)
    pair = lax.ppermute(shard, "dp", YLO_SWAP)
    shard = shard.astype(F32) + pair.astype(F32)
    grad_m = shard[24:28, :96]
    final = shard[:24].astype(BF16)
    final = lax.all_to_all(jnp.broadcast_to(final[None], (8, 24, 1152)), "dp", 0, 0, axis_index_groups=Z_GROUPS)
    final = final.reshape(4, 2, 24, 1152).transpose(0, 2, 1, 3).reshape(96, 2304).astype(F32)

    grads = grad_of_tokens(xs, dqs, dkvs, w_query, w_kv, w_merge)
    return attended[None], grads, final[:, :HD], final[:, HD:], grad_m


def solution(mesh):
    placed = (P("dp", "seq", None), P("dp", "seq"), P("dp", "seq", None), P(), P(), P())
    return jax.shard_map(
        on_device,
        mesh=mesh,
        in_specs=placed,
        out_specs=(
            P("dp", "seq", None),
            P("dp", "seq", None),
            P("seq", None),
            P("seq", None),
            P(None, "seq"),
        ),
        check_vma=False,
    )
```

time: 576 us -> 183 us (0.32)
  waiting for transfers between devices: 392 us -> 49.9 us
  blocking collectives: 77.2 us -> 26.8 us
  Pallas kernels: 0 us -> 50.2 us
  matrix products: 42.6 us -> 0 us
  starting transfers between devices: 0.65 us -> 43 us
  local copies, waits for them, and re-layouts: 35.5 us -> 7.84 us
  between operations: 14.6 us -> 1.08 us
  other arithmetic: 12.8 us -> 2.95 us
    unnamed x9 -> x0, waiting for transfers between devices: 211 us -> none
    reduce_scatter x1 -> x0, waiting for transfers between devices: 93.2 us -> none  [on_device(): lax.psum_scatter(term_kv.astype(jnp.bfloat16), 'seq', scatter_dimension=0...]
    all_gather x2 -> x0, waiting for transfers between devices: 87.1 us -> none  [the longest x1 44.8 us: on_device(): key_p = lax.all_gather(key, 'seq', axis=0, tiled=True)]
    psum x1 -> x0, blocking collectives: 77.2 us -> none  [on_device(): total_q, total_kv, total_m = lax.psum((slice_q, slice_kv, slice_m), 'dp')]
    pallas_call x0 -> x7, Pallas kernels: none -> 50.2 us  [the longest x1 21.1 us: attention(): pl.pallas_call(attention_kernel, in_specs=[smem()] + [vmem()] * 9, out_sp...]
    ppermute x0 -> x28, waiting for transfers between devices: none -> 49.9 us  [the longest x9 25.9 us: spread_x(): lax.ppermute(parts[k], 'seq', X_SHIFT[k])]
    dot_general x12 -> x0, matrix products: 42.6 us -> none  [the longest x1 8.37 us: on_device(): jnp.einsum('hqk,khd->hqd', expo.astype(jnp.bfloat16), value_h, preferred_...]
    ppermute x0 -> x28, starting transfers between devices: none -> 39.6 us  [the longest x9 14.2 us: spread_x(): lax.ppermute(parts[k], 'seq', X_SHIFT[k])]
  transfers between devices with their start and end apart: 6 -> 29, of which waited for: 6 -> 15; matrix products, arithmetic and copies ran while one was open for 8% -> 1% of each run, Pallas kernels for 0% -> 10%
where the time goes in v1:
time: 183 us; the launch traced here: 182 us
  Pallas kernels  50.2 us (27%)
  waiting for transfers between devices  49.9 us (27%)
  starting transfers between devices  43 us (23%)
  blocking collectives  26.8 us (15%)
  local copies, waits for them, and re-layouts  7.84 us (4%)
  other arithmetic  2.95 us (2%)
    all_to_all x1, blocking collectives, on_device(): got = lax.all_to_all(chunks, 'dp', 0, 0, axis_index_groups=Z_GROUPS)  26.8 us
    ppermute x9, waiting for transfers between devices, spread_x(): lax.ppermute(parts[k], 'seq', X_SHIFT[k])  25.9 us
    pallas_call x1, Pallas kernels, attention(): pl.pallas_call(attention_kernel, in_specs=[smem()] + [vmem()] * 9, out_sp...  21.1 us
    ppermute x9, starting transfers between devices, spread_x(): lax.ppermute(parts[k], 'seq', X_SHIFT[k])  14.2 us
    ppermute x1, waiting for transfers between devices, on_device(): m = m + lax.ppermute(m, 'seq', Y_SWAP)  9.26 us
    ppermute x3, starting transfers between devices, on_device(): dqs = [dq] + [lax.ppermute(dq, 'seq', X_SHIFT[k]) for k in range(1, 4)]  7.26 us
    pallas_call x1, Pallas kernels, grad_of_tokens(): pl.pallas_call(grad_tokens_kernel, grid_spec=grid_spec, out_shape=jax.Sha...  6.77 us
    pallas_call x1, Pallas kernels, keyval(): pl.pallas_call(keyval_kernel, grid=(6,), in_specs=[smem(), smem(), whole(...  6.29 us
  transfers between devices with their start and end apart: 29, of which 15 were waited for; matrix products, arithmetic and copies ran while one was open for 1% of the time, Pallas kernels for 10%

profile of v1, /device:TPU:2, one launch (start us, length us, event | category | flops | bytes accessed | tf_op | source)
XLA Modules:
  0.0 181.8 jit_solution(11818177452414130494)
XLA Ops:
  0.6 6.3 %keyval.1 = (bf16[3,64,128]{2,1,0:T(8,128)(2,1)}, bf16[3,64,128]{2,1,0:T(8,128)(2,1)}, bf16[3,64,128]{2,1,0:T(8,128)(2,1)}, bf16[3,64,128]{2,1,0:T(8,128)(2,1)}) custom-call(s32[1]{0:T(128)} %bitcast.x_ref, s32[256]{0:T(256)} %bitcast.58, f32[1,128]{1,0:T(1,128)} %constant.118.clone.freq_ref, bf16[256,1536]{1,0:T(8,128)(2,1)} %bitcast.41, f32[4,1536]{1,0:T(4,128)} %wm_ref.5, ...), custom_call_target="tpu_custom_call" | custom-call | tf_op jit(solution)/shard_map/keyval/pallas_call | solution.py:103
  6.9 1.5 collective-permute-start.3
  8.4 2.8 %collective-permute-start.4 = (bf16[3,64,128]{2,1,0:T(8,128)(2,1)}, bf16[3,64,128]{2,1,0:T(8,128)(2,1)S(1)}, u32[]{:S(2)}, u32[]{:S(2)}) collective-permute-start(bf16[3,64,128]{2,1,0:T(8,128)(2,1)} %get-tuple-element.30), channel_id=1, source_target_pairs={{0,8},{1,9},{2,10},{3,11},{4,12},{5,13},{6,14},{7,15},{8,0},{9,1},... | collective-permute-start | bytes 147464 | tf_op jit(solution)/shard_map/ppermute | solution.py:451
  11.3 0.4 collective-permute-start.5
  11.7 2.5 %collective-permute-done.4 = bf16[3,64,128]{2,1,0:T(8,128)(2,1)S(1)} collective-permute-done((bf16[3,64,128]{2,1,0:T(8,128)(2,1)}, bf16[3,64,128]{2,1,0:T(8,128)(2,1)S(1)}, u32[]{:S(2)}, u32[]{:S(2)}) %collective-permute-start.4) | collective-permute-done | bytes 49184 | tf_op jit(solution)/shard_map/ppermute | solution.py:451
  14.2 1.3 collective-permute-done.5
  15.6 0.8 pad_maximum_fusion.2.u0
  16.4 2.1 %collective-permute-start.6 = (bf16[4,3,64,128]{3,2,1,0:T(8,128)(2,1)S(1)}, bf16[4,3,64,128]{3,2,1,0:T(8,128)(2,1)S(1)}, u32[]{:S(2)}, u32[]{:S(2)}) collective-permute-start(bf16[4,3,64,128]{3,2,1,0:T(8,128)(2,1)S(1)} %pad_maximum_fusion.2.u0), channel_id=1, source_target_pairs={{0,2},{1,3},{2,0},{3,1},{4,6},{5,7},{6,4},{7,5},{8,10},{9,11},{10,... | collective-permute-start | bytes 589832 | tf_op jit(solution)/shard_map/ppermute | solution.py:468
  18.5 3.9 %queries.1 = (bf16[400,256]{1,0:T(8,128)(2,1)}, bf16[400,256]{1,0:T(8,128)(2,1)}, bf16[400,256]{1,0:T(8,128)(2,1)}, bf16[400,256]{1,0:T(8,128)(2,1)}) custom-call(s32[1]{0:T(128)} %bitcast.x_ref, s32[1,256]{1,0:T(1,128)} %idx_ref.1, f32[16,256]{1,0:T(8,128)} %constant.119.clone.freq_ref, bf16[256,1536]{1,0:T(8,128)(2,1)} %bitcast.42, ...), custom_call_target="tpu_custom_call" | custom-call | tf_op jit(solution)/shard_map/queries/pallas_call | solution.py:175
  22.4 1.1 collective-permute-start
  23.5 2.6 %collective-permute-start.1 = (bf16[400,256]{1,0:T(8,128)(2,1)}, bf16[400,256]{1,0:T(8,128)(2,1)S(1)}, u32[]{:S(2)}, u32[]{:S(2)}) collective-permute-start(bf16[400,256]{1,0:T(8,128)(2,1)} %get-tuple-element.26), channel_id=1, source_target_pairs={{0,8},{1,9},{2,10},{3,11},{4,12},{5,13},{6,14},{7,15},{8,0},{9,1},... | collective-permute-start | bytes 614408 | tf_op jit(solution)/shard_map/ppermute | solution.py:451
  26.1 2.0 %collective-permute-start.2 = (bf16[400,256]{1,0:T(8,128)(2,1)}, bf16[400,256]{1,0:T(8,128)(2,1)S(1)}, u32[]{:S(2)}, u32[]{:S(2)}) collective-permute-start(bf16[400,256]{1,0:T(8,128)(2,1)} %get-tuple-element.27), channel_id=1, source_target_pairs={{0,12},{1,13},{2,14},{3,15},{4,0},{5,1},{6,2},{7,3},{8,4},{9,5},{1... | collective-permute-start | bytes 614408 | tf_op jit(solution)/shard_map/ppermute | solution.py:451
  28.1 0.5 collective-permute-start.8
  28.6 1.6 collective-permute-done.q1
  30.2 2.1 %collective-permute-done.1.q2 = bf16[400,256]{1,0:T(8,128)(2,1)S(1)} collective-permute-done((bf16[400,256]{1,0:T(8,128)(2,1)}, bf16[400,256]{1,0:T(8,128)(2,1)S(1)}, u32[]{:S(2)}, u32[]{:S(2)}) %collective-permute-start.1) | collective-permute-done | bytes 204832 | tf_op jit(solution)/shard_map/ppermute | solution.py:451
  32.3 2.1 %collective-permute-done.2.q3 = bf16[400,256]{1,0:T(8,128)(2,1)S(1)} collective-permute-done((bf16[400,256]{1,0:T(8,128)(2,1)}, bf16[400,256]{1,0:T(8,128)(2,1)S(1)}, u32[]{:S(2)}, u32[]{:S(2)}) %collective-permute-start.2) | collective-permute-done | bytes 204832 | tf_op jit(solution)/shard_map/ppermute | solution.py:451
  34.4 0.6 copy-done.9
  35.1 0.1 copy-done.18
  35.2 21.1 %attention.1 = (bf16[192,256]{1,0:T(8,128)(2,1)}, bf16[192,256]{1,0:T(8,128)(2,1)}, bf16[192,256]{1,0:T(8,128)(2,1)}, bf16[192,256]{1,0:T(8,128)(2,1)}, bf16[4,1...) custom-call(s32[1]{0:T(128)} %bitcast.x_ref, f32[16,256]{1,0:T(8,128)} %constant.119.clone.freq_ref, ...), custom_call_target="tpu_custom_call" | custom-call | tf_op jit(solution)/shard_map/attention/pallas_call | solution.py:250
  56.3 0.1 collective-permute-start.15
  56.5 0.8 constant_dynamic-slice_fusion
  57.3 1.3 collective-permute-start.22
  58.7 0.4 collective-permute-start.16
  59.1 2.6 %collective-permute-start.14 = (bf16[4,192,256]{2,1,0:T(8,128)(2,1)S(1)}, bf16[4,192,256]{2,1,0:T(8,128)(2,1)S(1)}, u32[]{:S(2)}, u32[]{:S(2)}) collective-permute-start(bf16[4,192,256]{2,1,0:T(8,128)(2,1)S(1)} %copy-done.2), channel_id=1, source_target_pairs={{0,12},{1,13},{2,14},{3,15},{4,0},{5,1},{6,2},{7,3},{8,4},{9,5},{1... | collective-permute-start | bytes 1179656 | tf_op jit(solution)/shard_map/ppermute | solution.py:480
  61.7 3.5 %collective-permute-start.13 = (bf16[4,192,256]{2,1,0:T(8,128)(2,1)S(1)}, bf16[4,192,256]{2,1,0:T(8,128)(2,1)S(1)}, u32[]{:S(2)}, u32[]{:S(2)}) collective-permute-start(bf16[4,192,256]{2,1,0:T(8,128)(2,1)S(1)} %copy-done.2), channel_id=1, source_target_pairs={{0,8},{1,9},{2,10},{3,11},{4,12},{5,13},{6,14},{7,15},{8,0},{9,1},... | collective-permute-start | bytes 1179656 | tf_op jit(solution)/shard_map/ppermute | solution.py:480
  65.2 1.1 collective-permute-start.12
  66.3 0.8 collective-permute-done.16.y_ref
  67.1 2.4 %collective-permute-start.20 = (bf16[256,384]{1,0:T(8,128)(2,1)S(1)}, bf16[256,384]{1,0:T(8,128)(2,1)S(1)}, u32[]{:S(2)}, u32[]{:S(2)}) collective-permute-start(bf16[256,384]{1,0:T(8,128)(2,1)S(1)} %get-tuple-element.55), channel_id=1, source_target_pairs={{0,4},{1,5},{2,6},{3,7},{4,8},{5,9},{6,10},{7,11},{8,12},{9,13},{1... | collective-permute-start | bytes 589832 | tf_op jit(solution)/shard_map/ppermute | solution.py:451
  69.5 3.0 %finish_dkv.1.k0 = bf16[4,3,64,128]{3,2,1,0:T(8,128)(2,1)} custom-call(s32[1]{0:T(128)} %bitcast.x_ref, f32[1,128]{1,0:T(1,128)} %constant.118.clone.freq_ref, bf16[400,256]{1,0:T(8,128)(2,1)} %get-tuple-element.24.q0, bf16[400,256]{1,0:T(8,128)(2,1)} %copy-done.7, bf16[400,256]{1,0:T(8,128)(2,1)} %copy-done.8, bf16[400,256]{1,0:T(8,128)(2,1)} %copy-done.9, ...), custom_call_target="tpu_custom_call" | custom-call | tf_op jit(solution)/shard_map/finish_dkv/pallas_call | solution.py:290
  72.5 5.9 %collective-permute-done.21.t2 = bf16[256,384]{1,0:T(8,128)(2,1)S(1)} collective-permute-done((bf16[256,384]{1,0:T(8,128)(2,1)S(1)}, bf16[256,384]{1,0:T(8,128)(2,1)S(1)}, u32[]{:S(2)}, u32[]{:S(2)}) %collective-permute-start.21) | collective-permute-done | bytes 196640 | tf_op jit(solution)/shard_map/ppermute | solution.py:451
  78.4 10.4 %collective-permute-done.20.t1 = bf16[256,384]{1,0:T(8,128)(2,1)S(1)} collective-permute-done((bf16[256,384]{1,0:T(8,128)(2,1)S(1)}, bf16[256,384]{1,0:T(8,128)(2,1)S(1)}, u32[]{:S(2)}, u32[]{:S(2)}) %collective-permute-start.20) | collective-permute-done | bytes 196640 | tf_op jit(solution)/shard_map/ppermute | solution.py:451
  88.8 2.5 %collective-permute-start.18 = (bf16[4,3,64,128]{3,2,1,0:T(8,128)(2,1)}, bf16[4,3,64,128]{3,2,1,0:T(8,128)(2,1)S(1)}, u32[]{:S(2)}, u32[]{:S(2)}) collective-permute-start(bf16[4,3,64,128]{3,2,1,0:T(8,128)(2,1)} %finish_dkv.1.k0), channel_id=1, source_target_pairs={{0,8},{1,9},{2,10},{3,11},{4,12},{5,13},{6,14},{7,15},{8,0},{9,1},... | collective-permute-start | bytes 589832 | tf_op jit(solution)/shard_map/ppermute | solution.py:482
  91.3 2.0 %collective-permute-start.17 = (bf16[4,3,64,128]{3,2,1,0:T(8,128)(2,1)}, bf16[4,3,64,128]{3,2,1,0:T(8,128)(2,1)S(1)}, u32[]{:S(2)}, u32[]{:S(2)}) collective-permute-start(bf16[4,3,64,128]{3,2,1,0:T(8,128)(2,1)} %finish_dkv.1.k0), channel_id=1, source_target_pairs={{0,4},{1,5},{2,6},{3,7},{4,8},{5,9},{6,10},{7,11},{8,12},{9,13},{1... | collective-permute-start | bytes 589832 | tf_op jit(solution)/shard_map/ppermute | solution.py:482
  93.4 0.7 copy-done.4
  94.1 0.2 copy-done.5
  94.3 4.0 %term_q.1.tq_ref = f32[4,96,768]{2,1,0:T(8,128)} custom-call(s32[1]{0:T(128)} %bitcast.x_ref, bf16[256,384]{1,0:T(8,128)(2,1)} %get-tuple-element.56.t0, bf16[256,384]{1,0:T(8,128)(2,1)} %copy-done.16, bf16[256,384]{1,0:T(8,128)(2,1)} %copy-done.15, bf16[256,384]{1,0:T(8,128)(2,1)} %copy-done.14, bf16[4,192,256]{2,1,0:T(8,128)(2,1)} %get-tuple-element.36.d0, ...), custom_call_target="tpu_custom_call" | custom-call | tf_op jit(solution)/shard_map/term_q/pallas_call | solution.py:315
  98.4 3.2 %collective-permute-done.17.k1 = bf16[4,3,64,128]{3,2,1,0:T(8,128)(2,1)S(1)} collective-permute-done((bf16[4,3,64,128]{3,2,1,0:T(8,128)(2,1)}, bf16[4,3,64,128]{3,2,1,0:T(8,128)(2,1)S(1)}, u32[]{:S(2)}, u32[]{:S(2)}) %collective-permute-start.17) | collective-permute-done | bytes 196640 | tf_op jit(solution)/shard_map/ppermute | solution.py:482
  101.6 0.7 copy-done.13
  102.2 5.1 %term_kv.1 = (f32[2,96,2304]{2,1,0:T(8,128)}, bf16[2,96,2304]{2,1,0:T(8,128)(2,1)}, f32[8,384]{1,0:T(8,128)}) custom-call(s32[1]{0:T(128)} %bitcast.x_ref, s32[1]{0:T(128)} %bitcast.18.c_ref, bf16[256,384]{1,0:T(8,128)(2,1)} %get-tuple-element.56.t0, bf16[256,384]{1,0:T(8,128)(2,1)} %copy-done.16, bf16[256,384]{1,0:T(8,128)(2,1)} %copy-done.15, ...), custom_call_target="tpu_custom_call" | custom-call | tf_op jit(solution)/shard_map/term_kv/pallas_call | solution.py:388
  107.3 2.6 %collective-permute-done.23 = bf16[2,96,2304]{2,1,0:T(8,128)(2,1)S(1)} collective-permute-done((bf16[2,96,2304]{2,1,0:T(8,128)(2,1)}, bf16[2,96,2304]{2,1,0:T(8,128)(2,1)S(1)}, u32[]{:S(2)}, u32[]{:S(2)}) %collective-permute-start.23) | collective-permute-done | bytes 884768 | tf_op jit(solution)/shard_map/ppermute | solution.py:491
  110.0 1.6 convert_add_fusion
  111.7 3.1 %collective-permute-start.24 = (bf16[96,2304]{1,0:T(8,128)(2,1)S(1)}, bf16[96,2304]{1,0:T(8,128)(2,1)S(1)}, u32[]{:S(2)}, u32[]{:S(2)}) collective-permute-start(bf16[96,2304]{1,0:T(8,128)(2,1)S(1)} %fusion.1), channel_id=1, source_target_pairs={{0,2},{1,3},{2,0},{3,1},{4,6},{5,7},{6,4},{7,5},{8,10},{9,11},{10,... | collective-permute-start | bytes 1327112 | tf_op jit(solution)/shard_map/ppermute | solution.py:496
  114.7 1.2 collective-permute-done.25
  115.9 0.6 collective-permute-start.26
  116.5 9.3 %collective-permute-done.26 = f32[8,384]{1,0:T(8,128)S(1)} collective-permute-done((f32[8,384]{1,0:T(8,128)S(1)}, f32[8,384]{1,0:T(8,128)S(1)}, u32[]{:S(2)}, u32[]{:S(2)}) %collective-permute-start.26) | collective-permute-done | bytes 12320 | tf_op jit(solution)/shard_map/ppermute | solution.py:497
  125.7 0.1 fusion.2
  125.8 0.1 fusion
  125.9 0.1 reshape.33
  126.2 26.8 %all_to_all.10 = bf16[8,32,1152]{2,1,0:T(8,128)(2,1)S(1)} all-to-all(bf16[8,32,1152]{2,1,0:T(8,128)(2,1)S(1)} %pad_maximum_fusion), channel_id=1, replica_groups={{0,16,32,48,64,80,96,112},{128,144,160,176,192,208,224,240},{1,17,33,49..., dimensions={0} | all-to-all | bytes 1179648 | tf_op jit(solution)/shard_map/all_to_all | solution.py:503
  153.0 0.1 reduce_sum.12
  153.0 1.4 collective-permute-start.27
  154.5 3.0 %collective-permute-done.27 = bf16[32,1152]{1,0:T(8,128)(2,1)S(1)} collective-permute-done((bf16[32,1152]{1,0:T(8,128)(2,1)S(1)}, bf16[32,1152]{1,0:T(8,128)(2,1)S(1)}, u32[]{:S(2)}, u32[]{:S(2)}) %collective-permute-start.27) | collective-permute-done | bytes 73760 | tf_op jit(solution)/shard_map/ppermute | solution.py:505
  157.5 0.8 broadcast_in_dim.8
  158.3 3.5 %all-to-all-start.1 = ((bf16[8,24,1152]{2,1,0:T(8,128)(2,1)}), bf16[8,24,1152]{2,1,0:T(8,128)(2,1)S(1)}, u32[]{:S(2)}, u32[]{:S(2)}) async-start(bf16[8,24,1152]{2,1,0:T(8,128)(2,1)} %broadcast_in_dim.8), calls=%async_computation.1 | async-start | bytes 884736 | tf_op jit(solution)/shard_map/all_to_all | solution.py:509
  161.8 3.2 %collective-permute-start.9 = (bf16[192,256]{1,0:T(8,128)(2,1)S(1)}, bf16[192,256]{1,0:T(8,128)(2,1)S(1)}, u32[]{:S(2)}, u32[]{:S(2)}) collective-permute-start(bf16[192,256]{1,0:T(8,128)(2,1)S(1)} %copy-done.25), channel_id=1, source_target_pairs={{0,12},{1,13},{2,14},{3,15},{4,0},{5,1},{6,2},{7,3},{8,4},{9,5},{1... | collective-permute-start | bytes 294920 | tf_op jit(solution)/shard_map/ppermute | solution.py:484
  165.0 2.2 %collective-permute-start.11 = (bf16[192,256]{1,0:T(8,128)(2,1)S(1)}, bf16[192,256]{1,0:T(8,128)(2,1)S(1)}, u32[]{:S(2)}, u32[]{:S(2)}) collective-permute-start(bf16[192,256]{1,0:T(8,128)(2,1)S(1)} %copy-done.23), channel_id=1, source_target_pairs={{0,4},{1,5},{2,6},{3,7},{4,8},{5,9},{6,10},{7,11},{8,12},{9,13},{1... | collective-permute-start | bytes 294920 | tf_op jit(solution)/shard_map/ppermute | solution.py:484
  167.3 0.1 collective-permute-done.9
  167.4 3.8 %collective-permute-done.10 = bf16[192,256]{1,0:T(8,128)(2,1)S(1)} collective-permute-done((bf16[192,256]{1,0:T(8,128)(2,1)S(1)}, bf16[192,256]{1,0:T(8,128)(2,1)S(1)}, u32[]{:S(2)}, u32[]{:S(2)}) %collective-permute-start.10) | collective-permute-done | bytes 98336 | tf_op jit(solution)/shard_map/ppermute | solution.py:484
  171.3 0.9 copy.17
  172.2 6.8 %grad_tokens.1 = bf16[1,256,1536]{2,1,0:T(8,128)(2,1)} custom-call(s32[1]{0:T(128)} %bitcast.x_ref, bf16[4,192,256]{2,1,0:T(8,128)(2,1)} %get-tuple-element.36.d0, bf16[4,192,256]{2,1,0:T(8,128)(2,1)} %copy-done.5, bf16[4,192,256]{2,1,0:T(8,128)(2,1)} %copy-done.4, bf16[4,192,256]{2,1,0:T(8,128)(2,1)} %copy-done.3, bf16[4,3,64,128]{3,2,1,0:T(8,128)(2,1)} %finish_dkv.1.k0, ...), custom_call_target="tpu_custom_call" | custom-call | tf_op jit(solution)/shard_map/grad_tokens/pallas_call | solution.py:441
  179.0 0.6 slice.29
  179.6 0.5 copy.16
  180.2 0.7 slice.27
  180.9 0.9 slice.28
  (81 shorter events, 0.7 us)
Async XLA Ops:
  6.9 4.8 %collective-permute-start.3 = (bf16[3,64,128]{2,1,0:T(8,128)(2,1)}, bf16[3,64,128]{2,1,0:T(8,128)(2,1)S(1)}, u32[]{:S(2)}, u32[]{:S(2)}) collective-permute-start(bf16[3,64,128]{2,1,0:T(8,128)(2,1)} %get-tuple-element.29), channel_id=1, source_target_pairs={{0,4},{1,5},{2,6},{3,7},{4,8},{5,9},{6,10},{7,11},{8,12},{9,13},{1... | collective-permute-start | bytes 147464 | tf_op jit(solution)/shard_map/ppermute | solution.py:451
  8.4 5.8 %collective-permute-start.4 = (bf16[3,64,128]{2,1,0:T(8,128)(2,1)}, bf16[3,64,128]{2,1,0:T(8,128)(2,1)S(1)}, u32[]{:S(2)}, u32[]{:S(2)}) collective-permute-start(bf16[3,64,128]{2,1,0:T(8,128)(2,1)} %get-tuple-element.30), channel_id=1, source_target_pairs={{0,8},{1,9},{2,10},{3,11},{4,12},{5,13},{6,14},{7,15},{8,0},{9,1},... | collective-permute-start | bytes 147464 | tf_op jit(solution)/shard_map/ppermute | solution.py:451
  11.3 4.3 %collective-permute-start.5 = (bf16[3,64,128]{2,1,0:T(8,128)(2,1)}, bf16[3,64,128]{2,1,0:T(8,128)(2,1)S(1)}, u32[]{:S(2)}, u32[]{:S(2)}) collective-permute-start(bf16[3,64,128]{2,1,0:T(8,128)(2,1)} %get-tuple-element.31), channel_id=1, source_target_pairs={{0,12},{1,13},{2,14},{3,15},{4,0},{5,1},{6,2},{7,3},{8,4},{9,5},{1... | collective-permute-start | bytes 147464 | tf_op jit(solution)/shard_map/ppermute | solution.py:451
  16.4 11.7 %copy-start.10 = (bf16[4,3,64,128]{3,2,1,0:T(8,128)(2,1)}, bf16[4,3,64,128]{3,2,1,0:T(8,128)(2,1)S(1)}, u32[]{:S(2)}) copy-start(bf16[4,3,64,128]{3,2,1,0:T(8,128)(2,1)S(1)} %pad_maximum_fusion.2.u0) | copy-start | bytes 589828
  16.4 11.7 %collective-permute-start.6 = (bf16[4,3,64,128]{3,2,1,0:T(8,128)(2,1)S(1)}, bf16[4,3,64,128]{3,2,1,0:T(8,128)(2,1)S(1)}, u32[]{:S(2)}, u32[]{:S(2)}) collective-permute-start(bf16[4,3,64,128]{3,2,1,0:T(8,128)(2,1)S(1)} %pad_maximum_fusion.2.u0), channel_id=1, source_target_pairs={{0,2},{1,3},{2,0},{3,1},{4,6},{5,7},{6,4},{7,5},{8,10},{9,11},{10,... | collective-permute-start | bytes 589832 | tf_op jit(solution)/shard_map/ppermute | solution.py:468
  18.5 38.0 %copy-start = (bf16[1,256,1536]{2,1,0:T(8,128)(2,1)S(1)}, bf16[1,256,1536]{2,1,0:T(8,128)(2,1)}, u32[]{:S(2)}) copy-start(bf16[1,256,1536]{2,1,0:T(8,128)(2,1)} %param.8) | copy-start | bytes 2359300
  22.4 7.8 %collective-permute-start = (bf16[400,256]{1,0:T(8,128)(2,1)}, bf16[400,256]{1,0:T(8,128)(2,1)S(1)}, u32[]{:S(2)}, u32[]{:S(2)}) collective-permute-start(bf16[400,256]{1,0:T(8,128)(2,1)} %get-tuple-element.25), channel_id=1, source_target_pairs={{0,4},{1,5},{2,6},{3,7},{4,8},{5,9},{6,10},{7,11},{8,12},{9,13},{1... | collective-permute-start | bytes 614408 | tf_op jit(solution)/shard_map/ppermute | solution.py:451
  23.5 8.8 %collective-permute-start.1 = (bf16[400,256]{1,0:T(8,128)(2,1)}, bf16[400,256]{1,0:T(8,128)(2,1)S(1)}, u32[]{:S(2)}, u32[]{:S(2)}) collective-permute-start(bf16[400,256]{1,0:T(8,128)(2,1)} %get-tuple-element.26), channel_id=1, source_target_pairs={{0,8},{1,9},{2,10},{3,11},{4,12},{5,13},{6,14},{7,15},{8,0},{9,1},... | collective-permute-start | bytes 614408 | tf_op jit(solution)/shard_map/ppermute | solution.py:451
  26.1 8.3 %collective-permute-start.2 = (bf16[400,256]{1,0:T(8,128)(2,1)}, bf16[400,256]{1,0:T(8,128)(2,1)S(1)}, u32[]{:S(2)}, u32[]{:S(2)}) collective-permute-start(bf16[400,256]{1,0:T(8,128)(2,1)} %get-tuple-element.27), channel_id=1, source_target_pairs={{0,12},{1,13},{2,14},{3,15},{4,0},{5,1},{6,2},{7,3},{8,4},{9,5},{1... | collective-permute-start | bytes 614408 | tf_op jit(solution)/shard_map/ppermute | solution.py:451
  28.1 6.3 %collective-permute-start.7 = (bf16[4,3,64,128]{3,2,1,0:T(8,128)(2,1)S(1)}, bf16[4,3,64,128]{3,2,1,0:T(8,128)(2,1)S(1)}, u32[]{:S(2)}, u32[]{:S(2)}) collective-permute-start(bf16[4,3,64,128]{3,2,1,0:T(8,128)(2,1)S(1)} %pad_maximum_fusion.2.u0), channel_id=1, source_target_pairs={{0,1},{1,0},{2,3},{3,2},{4,5},{5,4},{6,7},{7,6},{8,9},{9,8},{10,11... | collective-permute-start | bytes 589832 | tf_op jit(solution)/shard_map/ppermute | solution.py:467
  28.1 6.3 %copy-start.17 = (bf16[4,3,64,128]{3,2,1,0:T(8,128)(2,1)}, bf16[4,3,64,128]{3,2,1,0:T(8,128)(2,1)S(1)}, u32[]{:S(2)}) copy-start(bf16[4,3,64,128]{3,2,1,0:T(8,128)(2,1)S(1)} %collective-permute-done.6.u1) | copy-start | bytes 589828
  28.1 6.3 %collective-permute-start.8 = (bf16[4,3,64,128]{3,2,1,0:T(8,128)(2,1)S(1)}, bf16[4,3,64,128]{3,2,1,0:T(8,128)(2,1)S(1)}, u32[]{:S(2)}, u32[]{:S(2)}) collective-permute-start(bf16[4,3,64,128]{3,2,1,0:T(8,128)(2,1)S(1)} %collective-permute-done.6.u1), channel_id=1, source_target_pairs={{0,1},{1,0},{2,3},{3,2},{4,5},{5,4},{6,7},{7,6},{8,9},{9,8},{10,11... | collective-permute-start | bytes 589832 | tf_op jit(solution)/shard_map/ppermute | solution.py:469
  30.2 4.2 %copy-start.7 = (bf16[400,256]{1,0:T(8,128)(2,1)}, bf16[400,256]{1,0:T(8,128)(2,1)S(1)}, u32[]{:S(2)}) copy-start(bf16[400,256]{1,0:T(8,128)(2,1)S(1)} %collective-permute-done.q1) | copy-start | bytes 614404
  32.3 2.1 %copy-start.8 = (bf16[400,256]{1,0:T(8,128)(2,1)}, bf16[400,256]{1,0:T(8,128)(2,1)S(1)}, u32[]{:S(2)}) copy-start(bf16[400,256]{1,0:T(8,128)(2,1)S(1)} %collective-permute-done.1.q2) | copy-start | bytes 614404
  34.4 0.7 copy-start.9
  34.4 0.7 copy-start.18
  34.4 0.8 copy-start.20
  56.3 2.3 %copy-start.1 = (f32[3,512,128]{2,1,0:T(8,128)S(1)}, f32[3,512,128]{2,1,0:T(8,128)}, u32[]{:S(2)}) copy-start(f32[3,512,128]{2,1,0:T(8,128)} %get-tuple-element.37.keep_ref) | copy-start | bytes 2359300
  56.3 2.7 %copy-start.2 = (bf16[4,192,256]{2,1,0:T(8,128)(2,1)S(1)}, bf16[4,192,256]{2,1,0:T(8,128)(2,1)}, u32[]{:S(2)}) copy-start(bf16[4,192,256]{2,1,0:T(8,128)(2,1)} %get-tuple-element.36.d0) | copy-start | bytes 1179652
  56.3 2.3 %collective-permute-start.15 = (bf16[3,512,128]{2,1,0:T(8,128)(2,1)}, bf16[3,512,128]{2,1,0:T(8,128)(2,1)S(1)}, u32[]{:S(2)}, u32[]{:S(2)}) collective-permute-start(bf16[3,512,128]{2,1,0:T(8,128)(2,1)} %get-tuple-element.38), channel_id=1, source_target_pairs={{0,1},{1,0},{2,3},{3,2},{4,5},{5,4},{6,7},{7,6},{8,9},{9,8},{10,11... | collective-permute-start | bytes 1179656 | tf_op jit(solution)/shard_map/ppermute | solution.py:477
  57.3 7.9 %collective-permute-start.22 = (bf16[256,384]{1,0:T(8,128)(2,1)S(1)}, bf16[256,384]{1,0:T(8,128)(2,1)S(1)}, u32[]{:S(2)}, u32[]{:S(2)}) collective-permute-start(bf16[256,384]{1,0:T(8,128)(2,1)S(1)} %get-tuple-element.53), channel_id=1, source_target_pairs={{0,12},{1,13},{2,14},{3,15},{4,0},{5,1},{6,2},{7,3},{8,4},{9,5},{1... | collective-permute-start | bytes 589832 | tf_op jit(solution)/shard_map/ppermute | solution.py:451
  58.6 10.9 %copy-start.6 = (bf16[3,512,128]{2,1,0:T(8,128)(2,1)}, bf16[3,512,128]{2,1,0:T(8,128)(2,1)S(1)}, u32[]{:S(2)}) copy-start(bf16[3,512,128]{2,1,0:T(8,128)(2,1)S(1)} %collective-permute-done.15.core_ref) | copy-start | bytes 1179652
  58.7 8.5 %collective-permute-start.16 = (bf16[3,256,128]{2,1,0:T(8,128)(2,1)S(1)}, bf16[3,256,128]{2,1,0:T(8,128)(2,1)S(1)}, u32[]{:S(2)}, u32[]{:S(2)}) collective-permute-start(bf16[3,256,128]{2,1,0:T(8,128)(2,1)S(1)} %add_convert_fusion), channel_id=1, source_target_pairs={{0,2},{1,3},{2,0},{3,1},{4,6},{5,7},{6,4},{7,5},{8,10},{9,11},{10,... | collective-permute-start | bytes 589832 | tf_op jit(solution)/shard_map/ppermute | solution.py:479
  59.1 32.3 %collective-permute-start.14 = (bf16[4,192,256]{2,1,0:T(8,128)(2,1)S(1)}, bf16[4,192,256]{2,1,0:T(8,128)(2,1)S(1)}, u32[]{:S(2)}, u32[]{:S(2)}) collective-permute-start(bf16[4,192,256]{2,1,0:T(8,128)(2,1)S(1)} %copy-done.2), channel_id=1, source_target_pairs={{0,12},{1,13},{2,14},{3,15},{4,0},{5,1},{6,2},{7,3},{8,4},{9,5},{1... | collective-permute-start | bytes 1179656 | tf_op jit(solution)/shard_map/ppermute | solution.py:480
  61.7 16.7 %collective-permute-start.21 = (bf16[256,384]{1,0:T(8,128)(2,1)S(1)}, bf16[256,384]{1,0:T(8,128)(2,1)S(1)}, u32[]{:S(2)}, u32[]{:S(2)}) collective-permute-start(bf16[256,384]{1,0:T(8,128)(2,1)S(1)} %get-tuple-element.54), channel_id=1, source_target_pairs={{0,8},{1,9},{2,10},{3,11},{4,12},{5,13},{6,14},{7,15},{8,0},{9,1},... | collective-permute-start | bytes 589832 | tf_op jit(solution)/shard_map/ppermute | solution.py:451
  61.7 31.7 %collective-permute-start.13 = (bf16[4,192,256]{2,1,0:T(8,128)(2,1)S(1)}, bf16[4,192,256]{2,1,0:T(8,128)(2,1)S(1)}, u32[]{:S(2)}, u32[]{:S(2)}) collective-permute-start(bf16[4,192,256]{2,1,0:T(8,128)(2,1)S(1)} %copy-done.2), channel_id=1, source_target_pairs={{0,8},{1,9},{2,10},{3,11},{4,12},{5,13},{6,14},{7,15},{8,0},{9,1},... | collective-permute-start | bytes 1179656 | tf_op jit(solution)/shard_map/ppermute | solution.py:480
  65.2 28.2 %copy-start.14 = (bf16[256,384]{1,0:T(8,128)(2,1)}, bf16[256,384]{1,0:T(8,128)(2,1)S(1)}, u32[]{:S(2)}) copy-start(bf16[256,384]{1,0:T(8,128)(2,1)S(1)} %collective-permute-done.22.t3) | copy-start | bytes 589828
  65.2 28.2 %collective-permute-start.12 = (bf16[4,192,256]{2,1,0:T(8,128)(2,1)S(1)}, bf16[4,192,256]{2,1,0:T(8,128)(2,1)S(1)}, u32[]{:S(2)}, u32[]{:S(2)}) collective-permute-start(bf16[4,192,256]{2,1,0:T(8,128)(2,1)S(1)} %copy-done.2), channel_id=1, source_target_pairs={{0,4},{1,5},{2,6},{3,7},{4,8},{5,9},{6,10},{7,11},{8,12},{9,13},{1... | collective-permute-start | bytes 1179656 | tf_op jit(solution)/shard_map/ppermute | solution.py:480
  67.1 2.4 %copy-start.19 = (bf16[3,256,128]{2,1,0:T(8,128)(2,1)}, bf16[3,256,128]{2,1,0:T(8,128)(2,1)S(1)}, u32[]{:S(2)}) copy-start(bf16[3,256,128]{2,1,0:T(8,128)(2,1)S(1)} %collective-permute-done.16.y_ref) | copy-start | bytes 589828
  67.1 21.7 %collective-permute-start.20 = (bf16[256,384]{1,0:T(8,128)(2,1)S(1)}, bf16[256,384]{1,0:T(8,128)(2,1)S(1)}, u32[]{:S(2)}, u32[]{:S(2)}) collective-permute-start(bf16[256,384]{1,0:T(8,128)(2,1)S(1)} %get-tuple-element.55), channel_id=1, source_target_pairs={{0,4},{1,5},{2,6},{3,7},{4,8},{5,9},{6,10},{7,11},{8,12},{9,13},{1... | collective-permute-start | bytes 589832 | tf_op jit(solution)/shard_map/ppermute | solution.py:451
  78.4 15.0 %copy-start.15 = (bf16[256,384]{1,0:T(8,128)(2,1)}, bf16[256,384]{1,0:T(8,128)(2,1)S(1)}, u32[]{:S(2)}) copy-start(bf16[256,384]{1,0:T(8,128)(2,1)S(1)} %collective-permute-done.21.t2) | copy-start | bytes 589828
  78.4 19.9 %collective-permute-start.19 = (bf16[4,3,64,128]{3,2,1,0:T(8,128)(2,1)}, bf16[4,3,64,128]{3,2,1,0:T(8,128)(2,1)S(1)}, u32[]{:S(2)}, u32[]{:S(2)}) collective-permute-start(bf16[4,3,64,128]{3,2,1,0:T(8,128)(2,1)} %finish_dkv.1.k0), channel_id=1, source_target_pairs={{0,12},{1,13},{2,14},{3,15},{4,0},{5,1},{6,2},{7,3},{8,4},{9,5},{1... | collective-permute-start | bytes 589832 | tf_op jit(solution)/shard_map/ppermute | solution.py:482
  88.8 4.6 %copy-start.16 = (bf16[256,384]{1,0:T(8,128)(2,1)}, bf16[256,384]{1,0:T(8,128)(2,1)S(1)}, u32[]{:S(2)}) copy-start(bf16[256,384]{1,0:T(8,128)(2,1)S(1)} %collective-permute-done.20.t1) | copy-start | bytes 589828
  88.8 9.5 %collective-permute-start.18 = (bf16[4,3,64,128]{3,2,1,0:T(8,128)(2,1)}, bf16[4,3,64,128]{3,2,1,0:T(8,128)(2,1)S(1)}, u32[]{:S(2)}, u32[]{:S(2)}) collective-permute-start(bf16[4,3,64,128]{3,2,1,0:T(8,128)(2,1)} %finish_dkv.1.k0), channel_id=1, source_target_pairs={{0,8},{1,9},{2,10},{3,11},{4,12},{5,13},{6,14},{7,15},{8,0},{9,1},... | collective-permute-start | bytes 589832 | tf_op jit(solution)/shard_map/ppermute | solution.py:482
  91.3 2.1 %copy-start.3 = (bf16[4,192,256]{2,1,0:T(8,128)(2,1)}, bf16[4,192,256]{2,1,0:T(8,128)(2,1)S(1)}, u32[]{:S(2)}) copy-start(bf16[4,192,256]{2,1,0:T(8,128)(2,1)S(1)} %collective-permute-done.14.d3) | copy-start | bytes 1179652
  91.3 10.2 %collective-permute-start.17 = (bf16[4,3,64,128]{3,2,1,0:T(8,128)(2,1)}, bf16[4,3,64,128]{3,2,1,0:T(8,128)(2,1)S(1)}, u32[]{:S(2)}, u32[]{:S(2)}) collective-permute-start(bf16[4,3,64,128]{3,2,1,0:T(8,128)(2,1)} %finish_dkv.1.k0), channel_id=1, source_target_pairs={{0,4},{1,5},{2,6},{3,7},{4,8},{5,9},{6,10},{7,11},{8,12},{9,13},{1... | collective-permute-start | bytes 589832 | tf_op jit(solution)/shard_map/ppermute | solution.py:482
  93.4 0.7 copy-start.4
  93.4 0.9 copy-start.5
  98.3 3.2 %copy-start.11 = (bf16[4,3,64,128]{3,2,1,0:T(8,128)(2,1)}, bf16[4,3,64,128]{3,2,1,0:T(8,128)(2,1)S(1)}, u32[]{:S(2)}) copy-start(bf16[4,3,64,128]{3,2,1,0:T(8,128)(2,1)S(1)} %collective-permute-done.19.k3) | copy-start | bytes 589828
  98.3 3.2 %copy-start.12 = (bf16[4,3,64,128]{3,2,1,0:T(8,128)(2,1)}, bf16[4,3,64,128]{3,2,1,0:T(8,128)(2,1)S(1)}, u32[]{:S(2)}) copy-start(bf16[4,3,64,128]{3,2,1,0:T(8,128)(2,1)S(1)} %collective-permute-done.18.k2) | copy-start | bytes 589828
  101.6 0.7 copy-start.13
  107.3 2.6 %collective-permute-start.23 = (bf16[2,96,2304]{2,1,0:T(8,128)(2,1)}, bf16[2,96,2304]{2,1,0:T(8,128)(2,1)S(1)}, u32[]{:S(2)}, u32[]{:S(2)}) collective-permute-start(bf16[2,96,2304]{2,1,0:T(8,128)(2,1)} %get-tuple-element.41), channel_id=1, source_target_pairs={{0,1},{1,0},{2,3},{3,2},{4,5},{5,4},{6,7},{7,6},{8,9},{9,8},{10,11... | collective-permute-start | bytes 2654216 | tf_op jit(solution)/shard_map/ppermute | solution.py:491
  110.0 4.8 %copy-start.22 = (f32[8,384]{1,0:T(8,128)S(1)}, f32[8,384]{1,0:T(8,128)}, u32[]{:S(2)}) copy-start(f32[8,384]{1,0:T(8,128)} %get-tuple-element.42) | copy-start | bytes 36868
  111.7 14.2 %collective-permute-start.24 = (bf16[96,2304]{1,0:T(8,128)(2,1)S(1)}, bf16[96,2304]{1,0:T(8,128)(2,1)S(1)}, u32[]{:S(2)}, u32[]{:S(2)}) collective-permute-start(bf16[96,2304]{1,0:T(8,128)(2,1)S(1)} %fusion.1), channel_id=1, source_target_pairs={{0,2},{1,3},{2,0},{3,1},{4,6},{5,7},{6,4},{7,5},{8,10},{9,11},{10,... | collective-permute-start | bytes 1327112 | tf_op jit(solution)/shard_map/ppermute | solution.py:496
  114.7 1.2 collective-permute-start.25
  115.9 9.8 %collective-permute-start.26 = (f32[8,384]{1,0:T(8,128)S(1)}, f32[8,384]{1,0:T(8,128)S(1)}, u32[]{:S(2)}, u32[]{:S(2)}) collective-permute-start(f32[8,384]{1,0:T(8,128)S(1)} %add.127), channel_id=1, source_target_pairs={{0,2},{1,3},{2,0},{3,1},{4,6},{5,7},{6,4},{7,5},{8,10},{9,11},{10,... | collective-permute-start | bytes 36872 | tf_op jit(solution)/shard_map/ppermute | solution.py:497
  126.2 35.6 %copy-start.25 = (bf16[192,256]{1,0:T(8,128)(2,1)S(1)}, bf16[192,256]{1,0:T(8,128)(2,1)}, u32[]{:S(2)}) copy-start(bf16[192,256]{1,0:T(8,128)(2,1)} %get-tuple-element.33) | copy-start | bytes 294916
  126.2 38.9 %copy-start.24 = (bf16[192,256]{1,0:T(8,128)(2,1)S(1)}, bf16[192,256]{1,0:T(8,128)(2,1)}, u32[]{:S(2)}) copy-start(bf16[192,256]{1,0:T(8,128)(2,1)} %get-tuple-element.34) | copy-start | bytes 294916
  126.2 38.9 %copy-start.23 = (bf16[192,256]{1,0:T(8,128)(2,1)S(1)}, bf16[192,256]{1,0:T(8,128)(2,1)}, u32[]{:S(2)}) copy-start(bf16[192,256]{1,0:T(8,128)(2,1)} %get-tuple-element.35) | copy-start | bytes 294916
  126.2 45.0 %copy-start.21 = (bf16[192,256]{1,0:T(8,128)(2,1)S(1)}, bf16[192,256]{1,0:T(8,128)(2,1)}, u32[]{:S(2)}) copy-start(bf16[192,256]{1,0:T(8,128)(2,1)} %get-tuple-element.32) | copy-start | bytes 294916
  153.0 4.4 %collective-permute-start.27 = (bf16[32,1152]{1,0:T(8,128)(2,1)S(1)}, bf16[32,1152]{1,0:T(8,128)(2,1)S(1)}, u32[]{:S(2)}, u32[]{:S(2)}) collective-permute-start(bf16[32,1152]{1,0:T(8,128)(2,1)S(1)} %reduce_sum.12), channel_id=1, source_target_pairs={{0,128},{16,144},{32,160},{48,176},{64,192},{80,208},{96,224},{112... | collective-permute-start | bytes 221192 | tf_op jit(solution)/shard_map/ppermute | solution.py:505
  158.3 21.2 %all-to-all-start.1 = ((bf16[8,24,1152]{2,1,0:T(8,128)(2,1)}), bf16[8,24,1152]{2,1,0:T(8,128)(2,1)S(1)}, u32[]{:S(2)}, u32[]{:S(2)}) async-start(bf16[8,24,1152]{2,1,0:T(8,128)(2,1)} %broadcast_in_dim.8), calls=%async_computation.1 | async-start | bytes 884736 | tf_op jit(solution)/shard_map/all_to_all | solution.py:509
  161.8 5.6 %collective-permute-start.9 = (bf16[192,256]{1,0:T(8,128)(2,1)S(1)}, bf16[192,256]{1,0:T(8,128)(2,1)S(1)}, u32[]{:S(2)}, u32[]{:S(2)}) collective-permute-start(bf16[192,256]{1,0:T(8,128)(2,1)S(1)} %copy-done.25), channel_id=1, source_target_pairs={{0,12},{1,13},{2,14},{3,15},{4,0},{5,1},{6,2},{7,3},{8,4},{9,5},{1... | collective-permute-start | bytes 294920 | tf_op jit(solution)/shard_map/ppermute | solution.py:484
  165.0 6.1 %collective-permute-start.10 = (bf16[192,256]{1,0:T(8,128)(2,1)S(1)}, bf16[192,256]{1,0:T(8,128)(2,1)S(1)}, u32[]{:S(2)}, u32[]{:S(2)}) collective-permute-start(bf16[192,256]{1,0:T(8,128)(2,1)S(1)} %copy-done.24), channel_id=1, source_target_pairs={{0,8},{1,9},{2,10},{3,11},{4,12},{5,13},{6,14},{7,15},{8,0},{9,1},... | collective-permute-start | bytes 294920 | tf_op jit(solution)/shard_map/ppermute | solution.py:484
  165.0 6.1 %collective-permute-start.11 = (bf16[192,256]{1,0:T(8,128)(2,1)S(1)}, bf16[192,256]{1,0:T(8,128)(2,1)S(1)}, u32[]{:S(2)}, u32[]{:S(2)}) collective-permute-start(bf16[192,256]{1,0:T(8,128)(2,1)S(1)} %copy-done.23), channel_id=1, source_target_pairs={{0,4},{1,5},{2,6},{3,7},{4,8},{5,9},{6,10},{7,11},{8,12},{9,13},{1... | collective-permute-start | bytes 294920 | tf_op jit(solution)/shard_map/ppermute | solution.py:484
